TPU v7x, 32 devices: a whole 2x2x4 slice. The times are simulated.
32 devices in a mesh: freq: 4 (over z), space: 8 (over y, x, core).
Axes of the slice: x: 2, y: 2, z: 4, core: 2. Of those that a mesh axis runs over, the one named last changes fastest.
Arguments:
- direct: bfloat16 [2, 512, 65536], P(None, 'freq', 'space'), may hold values from -6 to 6
- adjoint: bfloat16 [2, 512, 65536], P(None, 'freq', 'space'), may hold values from -3.0517578e-05 to 3.0517578e-05
- coupling: float32 [7, 65536], P(None, 'space'), may hold values from 0.25 to 2
- wall: int32 [65536], P('space'), may hold values 0 or 1
Outputs:
- modes: bfloat16 [2, 512, 65536], P(None, 'freq', 'space')
- reduced: float32 [2, 512, 512], replicated
All inputs are finite; a program needn't handle non-finite values. No bound on the sum of `wall` on one device may be relied on, other than what follows from the above.
Results may differ from a plain program's by a relative error of at most 0.007.
Values may be sent and summed in bfloat16 or wider, within the bound.
A program may use at most 128 MiB of HBM per device.

v0:
```python
import jax
import jax.numpy as jnp
from jax import lax
from jax.sharding import PartitionSpec as P

NY = 64
NZ = 64
ITERS = 2


def extended(block, sides, width):
    for axis, dim in sides:
        count = lax.axis_size(axis)
        forward = [(i, i + 1) for i in range(count - 1)]
        backward = [(target, source) for source, target in forward]
        low = lax.ppermute(
            lax.slice_in_dim(block, block.shape[dim] - width, None, axis=dim), axis, forward
        )
        high = lax.ppermute(lax.slice_in_dim(block, 0, width, axis=dim), axis, backward)
        block = jnp.concatenate([low, block, high], axis=dim)
    return block


def complex_product(left_re, left_im, right_re, right_im):
    highest = lax.Precision.HIGHEST
    out_re = jnp.dot(left_re, right_re, precision=highest) - jnp.dot(
        left_im, right_im, precision=highest
    )
    out_im = jnp.dot(left_re, right_im, precision=highest) + jnp.dot(
        left_im, right_re, precision=highest
    )
    return (out_re, out_im)


def newton_schulz(hank_re, hank_im):
    total = jnp.sum(hank_re * hank_re + hank_im * hank_im)
    factor = 2.0 / total
    inverse_re = factor * hank_re.T
    inverse_im = -factor * hank_im.T
    identity = jnp.eye(hank_re.shape[0], dtype=jnp.float32)
    for iteration in range(ITERS):
        prod_re, prod_im = complex_product(hank_re, hank_im, inverse_re, inverse_im)
        inverse_re, inverse_im = complex_product(
            inverse_re, inverse_im, 2.0 * identity - prod_re, -prod_im
        )
    return (inverse_re, inverse_im)


def apply_operator(padded, coupling_local, wall_local, span_z):
    inner = padded[:, 1:-1]
    width = inner.shape[2]
    zero_rows = jnp.zeros(inner.shape[:2] + (span_z,), inner.dtype)
    zero_one = zero_rows[:, :, :1]
    north = jnp.concatenate([inner[:, :, span_z:], zero_rows], 2)
    south = jnp.concatenate([zero_rows, inner[:, :, : width - span_z]], 2)
    east = jnp.concatenate([inner[:, :, 1:], zero_one], 2)
    west = jnp.concatenate([zero_one, inner[:, :, : width - 1]], 2)
    zpos = jnp.arange(width, dtype=jnp.int32) % span_z
    east = jnp.where(zpos == span_z - 1, jnp.zeros_like(east), east)
    west = jnp.where(zpos == 0, jnp.zeros_like(west), west)
    beside = coupling_local[1] * padded[:, 2:] + coupling_local[2] * padded[:, :-2]
    beside = beside + coupling_local[3] * north + coupling_local[4] * south
    beside = beside + coupling_local[5] * east + coupling_local[6] * west
    result = coupling_local[0] * inner - beside
    return jnp.where(wall_local == 1, inner.astype(result.dtype), result)


def paired_rows(values):
    return jnp.concatenate(
        [jnp.concatenate([values[0], values[1]], 1), jnp.concatenate([values[1], -values[0]], 1)], 0
    )


def mode_rows(bal_re, bal_im, responses):
    mapping = jnp.concatenate(
        [jnp.concatenate([bal_re.T, -bal_im.T], 1), jnp.concatenate([bal_im.T, bal_re.T], 1)], 0
    )
    stacked = jnp.concatenate([responses[0], responses[1]], 0)
    phi = jnp.dot(mapping, stacked, preferred_element_type=jnp.float32)
    return phi.reshape(2, responses.shape[1], responses.shape[2])


def shards(direct, adjoint, coupling, wall):
    local_cols = direct.shape[1]
    cells = direct.shape[2]
    plane = NY * NZ
    planes = cells // plane
    coupling_local = coupling.reshape(7, planes, plane)
    wall_local = wall.reshape(planes, plane)
    dir_ex, adj_ex = (
        lax.all_to_all(direct, "freq", split_axis=2, concat_axis=1, tiled=True),
        lax.all_to_all(adjoint, "freq", split_axis=2, concat_axis=1, tiled=True),
    )
    columns = dir_ex.shape[1]
    adj_cat = jnp.concatenate([adj_ex[0], adj_ex[1]], 1)
    hank_local = lax.dot_general(
        adj_cat, paired_rows(dir_ex), (((1,), (1,)), ((), ())), preferred_element_type=jnp.float32
    )
    adj_wide = adj_cat.astype(jnp.float32)
    scale_out = columns / 16.0
    padded = extended(direct.reshape(2 * local_cols, planes, plane), (("space", 1),), 1)
    image = apply_operator(padded, coupling_local, wall_local, NZ).reshape(2, local_cols, cells)
    image_ex = lax.all_to_all(
        image.astype(jnp.bfloat16), "freq", split_axis=2, concat_axis=1, tiled=True
    ).astype(image.dtype)
    part = lax.dot_general(
        adj_wide, paired_rows(image_ex), (((1,), (1,)), ((), ())), precision=lax.Precision.HIGHEST
    )
    hank, moment = lax.psum((hank_local, part), ("freq", "space"))
    inverse_re, inverse_im = newton_schulz(hank[:, :columns], hank[:, columns:])
    bal_re = inverse_re.astype(jnp.bfloat16)
    bal_im = inverse_im.astype(jnp.bfloat16)
    red_re, red_im = complex_product(
        moment[:, :columns],
        moment[:, columns:],
        bal_re.astype(jnp.float32),
        bal_im.astype(jnp.float32),
    )
    reduced = scale_out * jnp.stack([red_re, red_im], 0)
    phi_ex = mode_rows(bal_re, bal_im, dir_ex).astype(jnp.bfloat16)
    modes = lax.all_to_all(phi_ex, "freq", split_axis=1, concat_axis=2, tiled=True)
    return (modes, reduced)


def solution(mesh):
    return jax.shard_map(
        shards,
        mesh=mesh,
        in_specs=(P(None, "freq", "space"), P(None, "freq", "space"), P(None, "space"), P("space")),
        out_specs=(P(None, "freq", "space"), P()),
        check_vma=False,
    )
```

profile of v0, /device:TPU:0, one launch (start us, length us, event | category | flops | bytes accessed | tf_op | source)
XLA Modules:
  0.0 672.1 jit_solution(14410634813536917582)
XLA Ops:
  7.2 11.2 %copy.42 = bf16[2,128,8192]{1,0,2:T(2,128)(2,1)} copy(bf16[2,128,8192]{2,1,0:T(8,128)(2,1)} %param.5) | data formatting | bytes 8388608 | tf_op args[1]
  18.4 6.3 all-to-all-start
  24.7 7.8 %reshape.44 = bf16[256,2,4096]{2,1,0:T(2,128)(2,1)} reshape(bf16[2,128,8192]{2,1,0:T(8,128)(2,1)} %param.4) | data formatting | bytes 8388608 | tf_op jit(solution)/shard_map/reshape | solution.py:101
  32.5 10.5 %fusion.112 = (bf16[256,1,4096]{2,1,0:T(2,128)(2,1)S(1)}, bf16[256,1,4096]{2,1,0:T(2,128)(2,1)S(1)}) fusion(bf16[256,2,4096]{2,1,0:T(2,128)(2,1)} %reshape.44), kind=kLoop, calls=%fused_computation.130 | loop fusion | bytes 8388608 | tf_op jit(solution)/shard_map/slice | solution.py:19
  43.0 2.3 copy.52
  45.4 1.6 collective-permute-start
  47.0 3.6 copy.54
  50.6 4.4 collective-permute-start.1
  55.0 10.4 %fusion.110 = (bf16[256,2,4032]{2,1,0:T(2,128)(2,1)}, bf16[256,2,4032]{2,1,0:T(2,128)(2,1)}) fusion(bf16[256,2,4096]{2,1,0:T(2,128)(2,1)S(1)} %copy-done), kind=kLoop, calls=%fused_computation.128 | loop fusion | bytes 16515072 | tf_op jit(solution)/shard_map/slice | solution.py:54
  65.4 11.2 %copy.46 = bf16[2,128,8192]{1,0,2:T(2,128)(2,1)} copy(bf16[2,128,8192]{2,1,0:T(8,128)(2,1)} %param.4) | data formatting | bytes 8388608 | tf_op args[0]
  77.2 12.0 %fusion.111 = (bf16[256,2,4095]{2,1,0:T(2,128)(2,1)}, bf16[256,2,4095]{2,1,0:T(2,128)(2,1)}) fusion(bf16[256,2,4096]{2,1,0:T(2,128)(2,1)} %reshape.44), kind=kLoop, calls=%fused_computation.129 | loop fusion | bytes 16773120 | tf_op jit(solution)/shard_map/slice | solution.py:56
  89.2 28.9 %all-to-all-done = bf16[2,128,8192]{1,0,2:T(2,128)(2,1)} async-done(((bf16[2,128,8192]{1,0,2:T(2,128)(2,1)}), bf16[2,128,8192]{1,0,2:T(2,128)(2,1)}, u32[]{:S(2)}, u32[]{:S(2)}) %all-to-all-start) | async-done | bytes 4194336 | tf_op jit(solution)/shard_map/all_to_all | solution.py:92
  118.1 5.1 all-to-all-start.1
  123.4 6.4 copy.53
  129.8 8.5 %copy.55 = bf16[256,1,4096]{2,1,0:T(2,128)(2,1)} copy(bf16[256,1,4096]{2,0,1:T(8,128)(2,1)} %collective-permute-done.1) | data formatting | bytes 4194304 | tf_op jit(solution)/shard_map/ppermute | solution.py:16
  138.3 64.1 %fusion.9 = bf16[256,2,4096]{2,1,0:T(2,128)(2,1)} fusion(bf16[256,2,4096]{2,1,0:T(2,128)(2,1)S(1)} %copy-done.1, pred[2,4096]{1,0:T(4,128)(4,1)S(1)} %eq.27, pred[4096]{0:T(1024)(128)(4,1)S(1)} %get-tuple-element.26, pred[4096]{0:T(1024)(128)(4,1)S(1)} %get-tuple-element.25, bf16[256,1,4096]{2,1,0:T(2,128)(2,1)} %copy.55, ...), kind=kLoop, calls=%fused_computation.11 | loop fusion | flops 62914560 | bytes 29472768 | tf_op jit(solution)/shard_map/convert_element_type | solution.py:104
  202.4 7.8 %convert_element_type.76 = bf16[2,128,8192]{2,1,0:T(8,128)(2,1)} reshape(bf16[256,2,4096]{2,1,0:T(2,128)(2,1)} %fusion.9) | data formatting | bytes 8388608 | tf_op jit(solution)/shard_map/convert_element_type | solution.py:104
  210.3 11.2 %copy.56 = bf16[2,128,8192]{1,0,2:T(2,128)(2,1)} copy(bf16[2,128,8192]{2,1,0:T(8,128)(2,1)} %convert_element_type.76) | data formatting | bytes 8388608 | tf_op jit(solution)/shard_map/convert_element_type | solution.py:104
  221.5 5.1 all-to-all-start.3
  226.6 10.6 %all-reduce.7.cloned.1.call-start = ((), (), s32[]{:S(2)}) async-start(), calls=%async_computation.4 | async-start | bytes 8388608 | tf_op jit(solution)/shard_map/psum | solution.py:109
  237.2 2.7 copy.43
  239.9 1.6 fusion.113
  241.5 4.0 copy.44
  245.5 2.7 copy.45
  248.2 2.7 copy.47
  251.0 2.3 fusion.114
  253.3 2.9 copy.48
  256.2 4.5 copy.49
  260.8 1.6 bitcast_negate_fusion.2
  263.8 8.1 %fusion.10 = f32[512,1024]{1,0:T(8,128)} fusion(bf16[512,2048]{1,0:T(8,128)(2,1)} %bitcast_negate_fusion.2, bf16[512,2048]{1,0:T(8,128)(2,1)S(1)} %bitcast.59, bf16[512,2048]{1,0:T(8,128)(2,1)S(1)} %bitcast.53, bf16[512,2048]{1,0:T(8,128)(2,1)} %bitcast.63, bf16[512,2048]{1,0:T(8,128)(2,1)S(1)} %bitcast.61), kind=kOutput, calls=%fused_computation.12 | convolution fusion | flops 4336910336 | bytes 12582912 | tf_op jit(solution)/shard_map/dot_general | solution.py:96
  271.8 47.2 %all-to-all-done.3 = bf16[2,128,8192]{1,0,2:T(2,128)(2,1)} async-done(((bf16[2,128,8192]{1,0,2:T(2,128)(2,1)}), bf16[2,128,8192]{1,0,2:T(2,128)(2,1)}, u32[]{:S(2)}, u32[]{:S(2)}) %all-to-all-start.3) | async-done | bytes 4194336 | tf_op jit(solution)/shard_map/all_to_all | solution.py:103
  319.0 2.7 copy.57
  322.3 4.0 fusion.109
  326.3 5.5 copy.58
  331.7 4.8 bitcast_negate_fusion
  336.5 5.6 copy.59
  342.1 22.9 %fusion = f32[512,1024]{1,0:T(8,128)} fusion(f32[512,2048]{1,0:T(8,128)} %bitcast_negate_fusion, f32[512,2048]{1,0:T(8,128)} %bitcast.57, f32[512,2048]{1,0:T(8,128)} %bitcast.50, bf16[512,2048]{1,0:T(8,128)(2,1)} %bitcast.64, bf16[512,2048]{1,0:T(8,128)(2,1)S(1)} %bitcast.62), kind=kOutput, calls=%fused_computation | convolution fusion | flops 25790775296 | bytes 18874368 | tf_op jit(solution)/shard_map/dot_general | solution.py:106
  365.0 141.3 %all-reduce.7.cloned.1.call-done = (f32[512,1024]{1,0:T(8,128)}, f32[512,1024]{1,0:T(8,128)}) async-done(((f32[512,1024]{1,0:T(8,128)}, f32[512,1024]{1,0:T(8,128)}), (f32[512,1024]{1,0:T(8,128)}, f32[512,1024]{1,0:T(8,128)})) %all-reduce.7.cloned.1.call-update) | async-done | bytes 4194320 | tf_op jit(solution)/shard_map/psum | solution.py:109
  506.4 2.6 add_reduce_fusion
  509.6 3.4 fusion.38
  513.1 1.9 fusion.36
  514.9 1.9 select_subtract_fusion.1
  516.8 1.9 fusion.32
  518.7 1.9 fusion.59
  520.6 1.9 fusion.34
  522.5 2.1 fusion.62
  524.6 1.9 fusion.85
  526.4 1.9 fusion.53
  528.3 1.9 fusion.87
  530.2 1.9 fusion.67
  532.0 1.9 select_subtract_fusion
  533.9 1.9 fusion.115
  535.8 2.1 fusion.116
  537.9 1.9 fusion.68
  539.8 1.9 bitcast_negate_fusion.1
  541.7 4.6 fusion.22
  546.2 6.6 copy.50
  552.8 5.0 all-to-all-start.2
  558.8 1.1 fusion.66
  560.9 1.1 fusion.65
  561.9 1.6 maximum_multiply_fusion
  563.5 86.1 %all-to-all-done.2 = bf16[2,512,2048]{2,0,1:T(2,128)(2,1)} async-done(((bf16[2,512,2048]{2,0,1:T(2,128)(2,1)}), bf16[2,512,2048]{2,0,1:T(2,128)(2,1)}, u32[]{:S(2)}, u32[]{:S(2)}) %all-to-all-start.2) | async-done | bytes 4194336 | tf_op jit(solution)/shard_map/all_to_all | solution.py:121
  649.6 7.4 %copy.51 = bf16[2,128,4,2048]{3,2,1,0:T(4,128)(2,1)} copy(bf16[2,128,4,2048]{3,0,1,2:T(2,128)(2,1)} %bitcast.14) | data formatting | bytes 8388608 | tf_op jit(solution)/shard_map/all_to_all | solution.py:121
  657.0 7.7 %all_to_all.51 = bf16[2,128,8192]{2,1,0:T(8,128)(2,1)} reshape(bf16[2,128,4,2048]{3,2,1,0:T(4,128)(2,1)} %copy.51) | data formatting | bytes 8388608 | tf_op jit(solution)/shard_map/all_to_all | solution.py:121
  (42 shorter events, 4.7 us)
Async XLA Ops:
  18.4 99.7 %all-to-all-start = ((bf16[2,128,8192]{1,0,2:T(2,128)(2,1)}), bf16[2,128,8192]{1,0,2:T(2,128)(2,1)}, u32[]{:S(2)}, u32[]{:S(2)}) async-start(bf16[2,128,8192]{1,0,2:T(2,128)(2,1)} %copy.42), calls=%async_computation | async-start | bytes 8388608 | tf_op jit(solution)/shard_map/all_to_all | solution.py:92
  45.4 9.6 %copy-start = (bf16[256,2,4096]{2,1,0:T(2,128)(2,1)S(1)}, bf16[256,2,4096]{2,1,0:T(2,128)(2,1)}, u32[]{:S(2)}) copy-start(bf16[256,2,4096]{2,1,0:T(2,128)(2,1)} %reshape.44) | copy-start | bytes 12582916
  45.4 78.0 %collective-permute-start = (bf16[256,1,4096]{2,0,1:T(8,128)(2,1)S(1)}, bf16[256,1,4096]{2,0,1:T(8,128)(2,1)}, u32[]{:S(2)}, u32[]{:S(2)}) collective-permute-start(bf16[256,1,4096]{2,0,1:T(8,128)(2,1)S(1)} %copy.52), channel_id=1, source_target_pairs={{1,0},{2,1},{3,2},{4,3},{5,4},{6,5},{7,6},{9,8},{10,9},{11,10},{12... | collective-permute-start | bytes 6291464 | tf_op jit(solution)/shard_map/ppermute | solution.py:19
  50.6 79.3 %collective-permute-start.1 = (bf16[256,1,4096]{2,0,1:T(8,128)(2,1)}, bf16[256,1,4096]{2,0,1:T(8,128)(2,1)}, u32[]{:S(2)}, u32[]{:S(2)}) collective-permute-start(bf16[256,1,4096]{2,0,1:T(8,128)(2,1)} %copy.54), channel_id=1, source_target_pairs={{0,1},{1,2},{2,3},{3,4},{4,5},{5,6},{6,7},{8,9},{9,10},{10,11},{11... | collective-permute-start | bytes 6291464 | tf_op jit(solution)/shard_map/ppermute | solution.py:16
  65.4 11.2 %copy-start.10 = (f32[7,8192]{1,0:T(8,128)S(1)}, f32[7,8192]{1,0:T(8,128)}, u32[]{:S(2)}) copy-start(f32[7,8192]{1,0:T(8,128)} %param.6) | copy-start | bytes 688132
  65.4 11.8 %copy-start.11 = (s32[8192]{0:T(1024)S(1)}, s32[8192]{0:T(1024)}, u32[]{:S(2)}) copy-start(s32[8192]{0:T(1024)} %param.7) | copy-start | bytes 98308
  118.1 103.4 %all-to-all-start.1 = ((bf16[2,128,8192]{1,0,2:T(2,128)(2,1)}), bf16[2,128,8192]{1,0,2:T(2,128)(2,1)}, u32[]{:S(2)}, u32[]{:S(2)}) async-start(bf16[2,128,8192]{1,0,2:T(2,128)(2,1)} %copy.46), calls=%async_computation.1 | async-start | bytes 8388608 | tf_op jit(solution)/shard_map/all_to_all | solution.py:91
  129.8 8.5 %copy-start.1 = (bf16[256,2,4096]{2,1,0:T(2,128)(2,1)S(1)}, bf16[256,2,4096]{2,1,0:T(2,128)(2,1)}, u32[]{:S(2)}) copy-start(bf16[256,2,4096]{2,1,0:T(2,128)(2,1)} %reshape.44) | copy-start | bytes 12582916
  221.5 97.5 %all-to-all-start.3 = ((bf16[2,128,8192]{1,0,2:T(2,128)(2,1)}), bf16[2,128,8192]{1,0,2:T(2,128)(2,1)}, u32[]{:S(2)}, u32[]{:S(2)}) async-start(bf16[2,128,8192]{1,0,2:T(2,128)(2,1)} %copy.56), calls=%async_computation.3 | async-start | bytes 8388608 | tf_op jit(solution)/shard_map/all_to_all | solution.py:103
  226.6 279.8 %all-reduce.7.cloned.1.call-start = ((), (), s32[]{:S(2)}) async-start(), calls=%async_computation.4 | async-start | bytes 8388608 | tf_op jit(solution)/shard_map/psum | solution.py:109
  256.2 6.1 copy-start.4
  260.8 2.3 copy-start.6
  260.8 3.0 copy-start.8
  336.5 5.6 copy-start.9
  506.4 6.7 copy-start.2
  537.8 3.8 copy-start.5
  537.8 3.8 copy-start.7
  552.8 5.0 copy-start.3
  552.8 96.8 %all-to-all-start.2 = ((bf16[2,512,2048]{2,0,1:T(2,128)(2,1)}), bf16[2,512,2048]{2,0,1:T(2,128)(2,1)}, u32[]{:S(2)}, u32[]{:S(2)}) async-start(bf16[2,512,2048]{2,0,1:T(2,128)(2,1)} %copy.50), calls=%async_computation.2 | async-start | bytes 8388608 | tf_op jit(solution)/shard_map/all_to_all | solution.py:121
Sparse Core Ops, SparseCore 0:
  365.1 141.1 all-reduce.6
where the time goes:
time: 682 us; the launch traced here: 672 us
  waiting for transfers between devices  304 us (45%)
  local copies, waits for them, and re-layouts  168 us (25%)
  other arithmetic  75.1 us (11%)
  matrix products  71.5 us (10%)
  starting transfers between devices  38 us (6%)
  between operations  15.6 us (2%)
    psum x1, waiting for transfers between devices, shards(): hank, moment = lax.psum((hank_local, part), ('freq', 'space'))  141 us
    all_to_all x1, waiting for transfers between devices, shards(): lax.all_to_all(phi_ex, 'freq', split_axis=1, concat_axis=2, tiled=True)  86.1 us
    convert_element_type x1, other arithmetic, shards(): image.astype(jnp.bfloat16)  64.1 us
    all_to_all x1, waiting for transfers between devices, shards(): lax.all_to_all(image.astype(jnp.bfloat16), 'freq', split_axis=2, concat_a...  47.2 us
    all_to_all x1, waiting for transfers between devices, shards(): lax.all_to_all(adjoint, 'freq', split_axis=2, concat_axis=1, tiled=True)  28.9 us
    unnamed x26, local copies, waits for them, and re-layouts  23.8 us
    dot_general x1, matrix products, shards(): lax.dot_general(adj_wide, paired_rows(image_ex), (((1,), (1,)), ((), ()))...  22.9 us
    convert_element_type x2, local copies, waits for them, and re-layouts, shards(): image.astype(jnp.bfloat16)  19.1 us
  transfers between devices with their start and end apart: 7, of which 4 were waited for; matrix products, arithmetic and copies ran while one was open for 29% of the time, Pallas kernels for 0%

commit v1 on v0

v1 whole, which is shorter than its diff:
```python
import jax
import jax.numpy as jnp
from jax import lax
from jax.experimental import pallas as pl
from jax.experimental.pallas import tpu as pltpu
from jax.sharding import PartitionSpec as P

NY = 64
NZ = 64
ITERS = 2


def complex_product(left_re, left_im, right_re, right_im):
    high = lax.Precision.HIGH
    out_re = jnp.dot(left_re, right_re, precision=high) - jnp.dot(
        left_im, right_im, precision=high
    )
    out_im = jnp.dot(left_re, right_im, precision=high) + jnp.dot(
        left_im, right_re, precision=high
    )
    return (out_re, out_im)


def newton_schulz(hank_re, hank_im):
    total = jnp.sum(hank_re * hank_re + hank_im * hank_im)
    factor = 2.0 / total
    inverse_re = factor * hank_re.T
    inverse_im = -factor * hank_im.T
    identity = jnp.eye(hank_re.shape[0], dtype=jnp.float32)
    for iteration in range(ITERS):
        prod_re, prod_im = complex_product(hank_re, hank_im, inverse_re, inverse_im)
        inverse_re, inverse_im = complex_product(
            inverse_re, inverse_im, 2.0 * identity - prod_re, -prod_im
        )
    return (inverse_re, inverse_im)


def stencil_kernel(planes, width, weights_ref, field_ref, banded_ref, low_ref, high_ref, out_ref):
    wide = width + 2 * NZ

    def plane_of(p):
        if p < 0:
            return low_ref[...]
        if p >= planes:
            return high_ref[...]
        return field_ref[:, p * width : (p + 1) * width]

    for p in range(planes):
        span = slice(p * width, (p + 1) * width)

        def weight(i):
            return weights_ref[i : i + 1, span]

        inner = plane_of(p).astype(jnp.float32)
        after = banded_ref[:, p * wide + 2 * NZ : (p + 1) * wide].astype(jnp.float32)
        before = banded_ref[:, p * wide : p * wide + width].astype(jnp.float32)
        beside = weight(1) * plane_of(p + 1).astype(jnp.float32)
        beside += weight(2) * plane_of(p - 1).astype(jnp.float32)
        beside += weight(3) * after
        beside += weight(4) * before
        beside += weight(5) * pltpu.roll(inner, width - 1, 1)
        beside += weight(6) * pltpu.roll(inner, 1, 1)
        out_ref[:, span] = (weight(0) * inner - beside).astype(out_ref.dtype)


def apply_operator(field, banded, low, high, weights, planes):
    rows, cells = field.shape
    width = cells // planes
    wide = width + 2 * NZ
    block = 64
    return pl.pallas_call(
        lambda *refs: stencil_kernel(planes, width, *refs),
        out_shape=jax.ShapeDtypeStruct((rows, cells), jnp.bfloat16),
        grid=(rows // block,),
        in_specs=[
            pl.BlockSpec((7, cells), lambda i: (0, 0)),
            pl.BlockSpec((block, cells), lambda i: (i, 0)),
            pl.BlockSpec((block, planes * wide), lambda i: (i, 0)),
            pl.BlockSpec((block, width), lambda i: (i, 0)),
            pl.BlockSpec((block, width), lambda i: (i, 0)),
        ],
        out_specs=pl.BlockSpec((block, cells), lambda i: (i, 0)),
        cost_estimate=pl.CostEstimate(
            flops=rows * cells * 40, bytes_accessed=rows * cells * 10, transcendentals=0
        ),
    )(weights, field, banded, low, high)


def conj_moment(left, right, parts):
    gram = lax.dot_general(
        left, right, (((1,), (1,)), ((), ())), preferred_element_type=jnp.float32
    )
    cols = gram.shape[0] // (2 * parts)
    gram = gram.reshape(parts, 2, cols, parts, 2, cols)
    out_re = gram[:, 0, :, :, 0, :] + gram[:, 1, :, :, 1, :]
    out_im = gram[:, 0, :, :, 1, :] - gram[:, 1, :, :, 0, :]
    return jnp.stack([out_re.reshape(parts * cols, -1), out_im.reshape(parts * cols, -1)], 0)


def mapping_of(bal_re, bal_im, parts):
    cols = bal_re.shape[0] // parts
    top_re = bal_re.T.reshape(parts, 1, cols, parts, 1, cols)
    top_im = bal_im.T.reshape(parts, 1, cols, parts, 1, cols)
    upper = jnp.concatenate([top_re, -top_im], 4)
    lower = jnp.concatenate([top_im, top_re], 4)
    return jnp.concatenate([upper, lower], 1).reshape(2 * parts * cols, 2 * parts * cols)


def shards(direct, adjoint, coupling, wall):
    parts = lax.axis_size("freq")
    slabs = lax.axis_size("space")
    mine = lax.axis_index("freq")
    local_cols = direct.shape[1]
    cells = direct.shape[2]
    plane = NY * NZ
    planes = cells // plane
    width = plane // parts
    columns = parts * local_cols

    def exchange(values):
        pieces = values.reshape(2 * local_cols, planes, parts, width).transpose(2, 0, 1, 3)
        pieces = pieces.reshape(parts, 2 * local_cols, planes * width)
        pieces = lax.all_to_all(pieces, "freq", split_axis=0, concat_axis=0, tiled=True)
        return pieces.reshape(2 * columns, planes * width)

    dir_ex = exchange(direct)
    adj_ex = exchange(adjoint)

    up = [(i, i + 1) for i in range(slabs - 1)]
    low = lax.ppermute(dir_ex[:, (planes - 1) * width :], "space", up)
    high = lax.ppermute(dir_ex[:, :width], "space", [(b, a) for a, b in up])
    over = [(i, i + 1) for i in range(parts - 1)]
    field = dir_ex.reshape(2 * columns, planes, width)
    first = field[:, :, :NZ].reshape(2 * columns, planes * NZ)
    last = field[:, :, width - NZ :].reshape(2 * columns, planes * NZ)
    before = lax.ppermute(last, "freq", over).reshape(2 * columns, planes, NZ)
    after = lax.ppermute(first, "freq", [(b, a) for a, b in over])
    after = after.reshape(2 * columns, planes, NZ)
    banded = jnp.concatenate([before, field, after], 2).reshape(2 * columns, -1)

    pick = coupling.reshape(7, planes, parts, width)
    pick = lax.dynamic_index_in_dim(pick, mine, 2, False).reshape(7, planes * width)
    held = wall.reshape(planes, parts, width)
    held = lax.dynamic_index_in_dim(held, mine, 1, False).reshape(1, planes * width) == 1
    zpos = jnp.arange(planes * width, dtype=jnp.int32)[None] % NZ
    slot = jnp.arange(7, dtype=jnp.int32)[:, None]
    off = held | ((slot == 5) & (zpos == NZ - 1)) | ((slot == 6) & (zpos == 0))
    weights = jnp.where(slot == 0, jnp.where(held, 1.0, pick), jnp.where(off, 0.0, pick))

    image = apply_operator(dir_ex, banded, low, high, weights, planes)

    hank = lax.psum(conj_moment(adj_ex, dir_ex, parts), ("freq", "space"))
    moment = conj_moment(adj_ex, image, parts)
    hank, moment = lax.optimization_barrier((hank, moment))
    moment = lax.psum(moment, ("freq", "space"))
    inverse_re, inverse_im = newton_schulz(hank[0], hank[1])
    bal_re = inverse_re.astype(jnp.bfloat16)
    bal_im = inverse_im.astype(jnp.bfloat16)
    mapping = mapping_of(bal_re, bal_im, parts)
    phi = jnp.dot(mapping, dir_ex, preferred_element_type=jnp.float32).astype(jnp.bfloat16)
    phi = phi.reshape(parts, 2 * local_cols, planes * width)
    modes = lax.all_to_all(phi, "freq", split_axis=0, concat_axis=0, tiled=True)
    modes = modes.reshape(parts, 2 * local_cols, planes, width).transpose(1, 2, 0, 3)
    modes = modes.reshape(2, local_cols, cells)
    red_re, red_im = complex_product(
        moment[0], moment[1], bal_re.astype(jnp.float32), bal_im.astype(jnp.float32)
    )
    reduced = (columns / 16.0) * jnp.stack([red_re, red_im], 0)
    return (modes, reduced)


def solution(mesh):
    return jax.shard_map(
        shards,
        mesh=mesh,
        in_specs=(P(None, "freq", "space"), P(None, "freq", "space"), P(None, "space"), P("space")),
        out_specs=(P(None, "freq", "space"), P()),
        check_vma=False,
    )
```

time: 682 us -> 684 us (level)
  waiting for transfers between devices: 304 us -> 404 us
  local copies, waits for them, and re-layouts: 168 us -> 128 us
  other arithmetic: 75.1 us -> 38.4 us
  matrix products: 71.5 us -> 49.5 us
  Pallas kernels: 0 us -> 15 us
  starting transfers between devices: 38 us -> 24.2 us
    psum x1 -> x2, waiting for transfers between devices: 141 us -> 273 us  [the longest x1 203 us: shards(): moment = lax.psum(moment, ('freq', 'space'))]
    reshape x1 -> x16, local copies, waits for them, and re-layouts: 7.85 us -> 80.9 us  [the longest x2 17.6 us: shards(): modes.reshape(parts, 2 * local_cols, planes, width).transpose(1, 2, 0, 3)]
    slice x15 -> x3, local copies, waits for them, and re-layouts: 72.6 us -> 6.82 us  [the longest x1 4.68 us: shards(): high = lax.ppermute(dir_ex[:, :width], 'space', [(b, a) for a, b in up])]
    convert_element_type x2 -> x0, other arithmetic: 64.7 us -> none  [the longest x1 64.1 us: shards(): image.astype(jnp.bfloat16)]
    all_to_all x4 -> x3, waiting for transfers between devices: 162 us -> 130 us  [the longest x2 130 us: exchange(): lax.all_to_all(pieces, 'freq', split_axis=0, concat_axis=0, tiled=True)]
    convert_element_type x3 -> x0, local copies, waits for them, and re-layouts: 25.6 us -> none  [the longest x2 19.1 us: shards(): image.astype(jnp.bfloat16)]
    all_to_all x5 -> x0, local copies, waits for them, and re-layouts: 23.4 us -> none  [the longest x2 15.2 us: shards(): lax.all_to_all(phi_ex, 'freq', split_axis=1, concat_axis=2, tiled=True)]
    unnamed x26 -> x11, local copies, waits for them, and re-layouts: 23.8 us -> 1.48 us
  transfers between devices with their start and end apart: 7 -> 9, of which waited for: 4 -> 4; matrix products, arithmetic and copies ran while one was open for 29% -> 17% of each run, Pallas kernels for 0% -> 2%
where the time goes in v1:
time: 684 us; the launch traced here: 674 us
  waiting for transfers between devices  404 us (59%)
  local copies, waits for them, and re-layouts  128 us (19%)
  matrix products  49.5 us (7%)
  other arithmetic  38.4 us (6%)
  starting transfers between devices  24.2 us (4%)
  between operations  15.6 us (2%)
  Pallas kernels  15 us (2%)
    psum x1, waiting for transfers between devices, shards(): moment = lax.psum(moment, ('freq', 'space'))  203 us
    all_to_all x2, waiting for transfers between devices, exchange(): lax.all_to_all(pieces, 'freq', split_axis=0, concat_axis=0, tiled=True)  130 us
    psum x1, waiting for transfers between devices, shards(): hank = lax.psum(conj_moment(adj_ex, dir_ex, parts), ('freq', 'space'))  69.7 us
    another operation x2, local copies, waits for them, and re-layouts, shards(): field = dir_ex.reshape(2 * columns, planes, width)  19 us
    add x2, other arithmetic, conj_moment(): out_re = gram[:, 0, :, :, 0, :] + gram[:, 1, :, :, 1, :]  18.6 us
    dot_general x2, matrix products, conj_moment(): lax.dot_general(left, right, (((1,), (1,)), ((), ())), preferred_element_...  17.6 us
    reshape x2, local copies, waits for them, and re-layouts, shards(): modes.reshape(parts, 2 * local_cols, planes, width).transpose(1, 2, 0, 3)  17.6 us
    reshape x2, local copies, waits for them, and re-layouts, exchange(): values.reshape(2 * local_cols, planes, parts, width).transpose(2, 0, 1, 3)  15.6 us
  transfers between devices with their start and end apart: 9, of which 4 were waited for; matrix products, arithmetic and copies ran while one was open for 17% of the time, Pallas kernels for 2%

profile of v1, /device:TPU:0, one launch (start us, length us, event | category | flops | bytes accessed | tf_op | source)
XLA Modules:
  0.0 673.9 jit_solution(18017488965381104955)
XLA Ops:
  7.2 7.8 %reshape.205 = bf16[256,2,4,1024]{3,2,1,0:T(4,128)(2,1)} reshape(bf16[2,128,8192]{2,1,0:T(8,128)(2,1)} %param.4) | data formatting | bytes 8388608 | tf_op jit(solution)/shard_map/reshape | solution.py:121
  15.0 7.4 %copy.24 = bf16[4,256,2,1024]{3,2,1,0:T(2,128)(2,1)} copy(bf16[4,256,2,1024]{3,0,2,1:T(4,128)(2,1)} %bitcast.128) | data formatting | bytes 8388608 | tf_op jit(solution)/shard_map/transpose | solution.py:121
  22.4 7.8 %reshape.206 = bf16[4,256,2048]{2,1,0:T(8,128)(2,1)} reshape(bf16[4,256,2,1024]{3,2,1,0:T(2,128)(2,1)} %copy.24) | data formatting | bytes 8388608 | tf_op jit(solution)/shard_map/reshape | solution.py:122
  30.1 6.3 all-to-all-start.1
  36.5 7.8 %reshape.203 = bf16[256,2,4,1024]{3,2,1,0:T(4,128)(2,1)} reshape(bf16[2,128,8192]{2,1,0:T(8,128)(2,1)} %param.5) | data formatting | bytes 8388608 | tf_op jit(solution)/shard_map/reshape | solution.py:121
  44.3 7.4 %copy.23 = bf16[4,256,2,1024]{3,2,1,0:T(2,128)(2,1)} copy(bf16[4,256,2,1024]{3,0,2,1:T(4,128)(2,1)} %bitcast.129) | data formatting | bytes 8388608 | tf_op jit(solution)/shard_map/transpose | solution.py:121
  51.7 7.8 %reshape.204 = bf16[4,256,2048]{2,1,0:T(8,128)(2,1)} reshape(bf16[4,256,2,1024]{3,2,1,0:T(2,128)(2,1)} %copy.23) | data formatting | bytes 8388608 | tf_op jit(solution)/shard_map/reshape | solution.py:122
  59.4 70.5 %all-to-all-done.1 = bf16[4,256,2048]{2,1,0:T(8,128)(2,1)} async-done(((bf16[4,256,2048]{2,1,0:T(8,128)(2,1)}), bf16[4,256,2048]{2,1,0:T(8,128)(2,1)}, u32[]{:S(2)}, u32[]{:S(2)}) %all-to-all-start.1) | async-done | bytes 4194336 | tf_op jit(solution)/shard_map/all_to_all | solution.py:123
  129.9 4.9 all-to-all-start
  136.1 7.8 %reshape.226 = bf16[1024,2,1024]{2,1,0:T(2,128)(2,1)} reshape(bf16[4,256,2048]{2,1,0:T(8,128)(2,1)} %all-to-all-done.1) | data formatting | bytes 8388608 | tf_op jit(solution)/shard_map/reshape;reshape | solution.py:133
  143.9 11.2 %copy.38 = bf16[1024,2,1024]{0,2,1:T(8,128)(2,1)} copy(bf16[1024,2,1024]{2,1,0:T(2,128)(2,1)} %reshape.226) | data formatting | bytes 8388608 | tf_op jit(solution)/shard_map/reshape;reshape | solution.py:133
  155.1 1.1 fusion.74
  156.2 3.8 collective-permute-start
  160.0 1.3 collective-permute-start.1
  161.3 4.7 fusion.73
  166.0 1.4 collective-permute-start.2
  167.4 1.5 collective-permute-start.3
  169.0 59.5 %all-to-all-done = bf16[4,256,2048]{2,1,0:T(8,128)(2,1)} async-done(((bf16[4,256,2048]{2,1,0:T(8,128)(2,1)}), bf16[4,256,2048]{2,1,0:T(8,128)(2,1)}, u32[]{:S(2)}, u32[]{:S(2)}) %all-to-all-start) | async-done | bytes 4194336 | tf_op jit(solution)/shard_map/all_to_all | solution.py:123
  228.4 7.6 %fusion.75 = f32[4,2,128,4,2,128]{5,2,4,3,1,0:T(8,128)S(1)} fusion(bf16[4,2,128,2048,1,1]{3,2,5,4,1,0:T(8,128)(2,1)} %bitcast.3, bf16[4,2,128,2048,1,1]{3,2,1,0,5,4:T(8,128)(2,1)} %bitcast.7), kind=kOutput, calls=%fused_computation.96 | convolution fusion | flops 4294967296 | bytes 12582912 | tf_op jit(solution)/shard_map/dot_general | solution.py:90
  237.6 3.2 pad_maximum_fusion.1
  240.9 4.0 pad_maximum_fusion
  244.9 6.7 copy.39.refs_2_
  251.6 1.4 copy-done.2
  253.0 15.0 %shard_map.59 = bf16[1024,2048]{1,0:T(8,128)(2,1)} custom-call(f32[7,2048]{1,0:T(8,128)} %select_select_fusion.refs_0_, bf16[1024,2048]{1,0:T(8,128)(2,1)} %bitcast.10.refs_1_, bf16[1024,2304]{1,0:T(8,128)(2,1)} %copy.39.refs_2_, bf16[1024,1024]{1,0:T(8,128)(2,1)} %copy-done.2, bf16[1024,1024]{1,0:T(8,128)(2,1)} %collective-permute-done.3.refs_4_), custom_call_target="tpu_custom_call" | custom-call | flops 83886080 | bytes 20971520 | tf_op jit(solution)/shard_map/pallas_call | solution.py:71
  268.0 10.0 %convolution_bitcast_fusion = f32[1024,1024]{0,1:T(8,128)} fusion(bf16[1024,2048]{1,0:T(8,128)(2,1)} %shard_map.59, bf16[1024,2048]{1,0:T(8,128)(2,1)} %bitcast.16), kind=kOutput, calls=%fused_computation.3 | convolution fusion | flops 4294967296 | bytes 12582912 | tf_op jit(solution)/shard_map/dot_general | solution.py:90
  278.0 6.6 reshape.217
  284.6 18.4 %fusion.39 = (f32[4,128,4,128]{1,0,3,2:T(4,128)S(1)}, f32[4,128,4,128]{1,0,3,2:T(4,128)S(1)}) fusion(f32[4,2,128,4,2,128]{2,1,0,5,4,3:T(2,128)} %reshape.217), kind=kLoop, calls=%fused_computation.48 | loop fusion | flops 524288 | bytes 6291456 | tf_op jit(solution)/shard_map/add | solution.py:95
  303.8 1.5 pad_maximum_fusion.2
  305.3 69.7 %all-reduce.3.cloned.1.call-done = f32[2,512,512]{2,0,1:T(2,128)} async-done(((f32[2,512,512]{2,0,1:T(2,128)}), f32[2,512,512]{2,0,1:T(2,128)}) %all-reduce.3.cloned.1.call-update) | async-done | bytes 2097168 | tf_op jit(solution)/shard_map/psum | solution.py:152
  375.0 2.1 copy.30
  377.2 1.1 slice.61
  378.3 0.9 fusion.48
  379.9 1.0 fusion.6
  380.9 1.0 fusion.4
  381.9 1.1 select_subtract_fusion.1
  383.0 1.1 fusion
  384.1 1.0 fusion.27
  385.1 1.0 fusion.2
  386.2 1.0 fusion.30
  387.2 1.0 fusion.51
  388.3 1.3 fusion.21
  389.6 1.0 fusion.52
  390.6 1.0 fusion.35
  391.6 1.0 select_subtract_fusion
  392.7 1.0 fusion.76
  393.7 1.0 fusion.77
  394.8 1.1 fusion.36
  395.9 1.1 fusion.37
  397.1 1.5 copy.31
  398.6 1.1 neg.23
  399.7 0.9 reshape.218
  400.6 3.8 copy.32
  404.3 6.7 maximum_maximum_fusion
  411.1 4.7 reshape.220
  415.7 9.3 %convolution_convert_fusion = bf16[1024,2048]{1,0:T(8,128)(2,1)} fusion(bf16[1024,1024]{1,0:T(8,128)(2,1)} %reshape.220, bf16[1024,2048]{1,0:T(8,128)(2,1)} %bitcast.10.refs_1_), kind=kOutput, calls=%fused_computation.2 | convolution fusion | flops 4297064448 | bytes 10485760 | tf_op jit(solution)/shard_map/dot_general | solution.py:160
  425.1 4.8 all-to-all-start.2
  430.7 203.3 %all-reduce.5.cloned.1.call-done = f32[2,512,512]{1,2,0:T(8,128)} async-done(((f32[2,512,512]{1,2,0:T(8,128)}), f32[2,512,512]{1,2,0:T(8,128)}) %all-reduce.5.cloned.1.call-update) | async-done | bytes 2097168 | tf_op jit(solution)/shard_map/psum | solution.py:155
  634.0 2.1 fusion.50
  636.1 2.0 fusion.34
  638.9 0.8 fusion.33
  639.6 1.6 maximum_multiply_fusion
  641.2 8.1 %reshape.222 = bf16[4,256,2,1024]{3,2,1,0:T(2,128)(2,1)} reshape(bf16[4,256,2048]{2,1,0:T(8,128)(2,1)} %all-to-all-done.2) | data formatting | bytes 8388608 | tf_op jit(solution)/shard_map/reshape | solution.py:163
  649.3 9.5 %copy.75 = bf16[4,256,2,1024]{3,0,2,1:T(4,128)(2,1)} copy(bf16[4,256,2,1024]{3,2,1,0:T(2,128)(2,1)} %reshape.222) | data formatting | bytes 8388608 | tf_op jit(solution)/shard_map/reshape | solution.py:163
  658.8 7.8 %reshape.223 = bf16[2,128,8192]{2,1,0:T(8,128)(2,1)} reshape(bf16[256,2,4,1024]{3,2,1,0:T(4,128)(2,1)} %bitcast.127) | data formatting | bytes 8388608 | tf_op jit(solution)/shard_map/reshape | solution.py:164
  (35 shorter events, 5.4 us)
Async XLA Ops:
  30.1 99.8 %all-to-all-start.1 = ((bf16[4,256,2048]{2,1,0:T(8,128)(2,1)}), bf16[4,256,2048]{2,1,0:T(8,128)(2,1)}, u32[]{:S(2)}, u32[]{:S(2)}) async-start(bf16[4,256,2048]{2,1,0:T(8,128)(2,1)} %reshape.206), calls=%async_computation.1 | async-start | bytes 8388608 | tf_op jit(solution)/shard_map/all_to_all | solution.py:123
  59.4 75.4 %copy-start.3 = (f32[7,8192]{1,0:T(8,128)S(1)}, f32[7,8192]{1,0:T(8,128)}, u32[]{:S(2)}) copy-start(f32[7,8192]{1,0:T(8,128)} %param.6) | copy-start | bytes 688132
  59.4 75.8 %copy-start.4 = (s32[8192]{0:T(1024)S(1)}, s32[8192]{0:T(1024)}, u32[]{:S(2)}) copy-start(s32[8192]{0:T(1024)} %param.7) | copy-start | bytes 98308
  129.9 98.5 %all-to-all-start = ((bf16[4,256,2048]{2,1,0:T(8,128)(2,1)}), bf16[4,256,2048]{2,1,0:T(8,128)(2,1)}, u32[]{:S(2)}, u32[]{:S(2)}) async-start(bf16[4,256,2048]{2,1,0:T(8,128)(2,1)} %reshape.204), calls=%async_computation | async-start | bytes 8388608 | tf_op jit(solution)/shard_map/all_to_all | solution.py:123
  134.8 240.2 %all-reduce.3.cloned.1.call-start = ((), (), s32[]{:S(2)}) async-start(), calls=%async_computation.3 | async-start | bytes 4194304 | tf_op jit(solution)/shard_map/psum | solution.py:152
  156.2 84.7 %collective-permute-start = (bf16[1024,128]{0,1:T(8,128)(2,1)S(1)}, bf16[1024,128]{0,1:T(8,128)(2,1)S(1)}, u32[]{:S(2)}, u32[]{:S(2)}) collective-permute-start(bf16[1024,128]{0,1:T(8,128)(2,1)S(1)} %bitcast.139), channel_id=1, source_target_pairs={{0,8},{8,16},{16,24},{1,9},{9,17},{17,25},{2,10},{10,18},{18,26},{... | collective-permute-start | bytes 786440 | tf_op jit(solution)/shard_map/ppermute | solution.py:136
  160.0 80.9 %collective-permute-start.1 = (bf16[1024,128]{0,1:T(8,128)(2,1)S(1)}, bf16[1024,128]{0,1:T(8,128)(2,1)S(1)}, u32[]{:S(2)}, u32[]{:S(2)}) collective-permute-start(bf16[1024,128]{0,1:T(8,128)(2,1)S(1)} %bitcast.138), channel_id=1, source_target_pairs={{8,0},{16,8},{24,16},{9,1},{17,9},{25,17},{10,2},{18,10},{26,18},{... | collective-permute-start | bytes 786440 | tf_op jit(solution)/shard_map/ppermute | solution.py:137
  166.0 85.6 %collective-permute-start.2 = (bf16[1024,1024]{1,0:T(8,128)(2,1)}, bf16[1024,1024]{1,0:T(8,128)(2,1)S(1)}, u32[]{:S(2)}, u32[]{:S(2)}) collective-permute-start(bf16[1024,1024]{1,0:T(8,128)(2,1)} %get-tuple-element.9), channel_id=1, source_target_pairs={{0,1},{1,2},{2,3},{3,4},{4,5},{5,6},{6,7},{8,9},{9,10},{10,11},{11... | collective-permute-start | bytes 6291464 | tf_op jit(solution)/shard_map/ppermute | solution.py:130
  167.4 84.2 %collective-permute-start.3 = (bf16[1024,1024]{1,0:T(8,128)(2,1)}, bf16[1024,1024]{1,0:T(8,128)(2,1)}, u32[]{:S(2)}, u32[]{:S(2)}) collective-permute-start(bf16[1024,1024]{1,0:T(8,128)(2,1)} %get-tuple-element.8), channel_id=1, source_target_pairs={{1,0},{2,1},{3,2},{4,3},{5,4},{6,5},{7,6},{9,8},{10,9},{11,10},{12... | collective-permute-start | bytes 6291464 | tf_op jit(solution)/shard_map/ppermute | solution.py:131
  251.6 1.4 copy-start.2
  375.0 2.2 copy-start.1
  425.1 216.1 %all-to-all-start.2 = ((bf16[4,256,2048]{2,1,0:T(8,128)(2,1)}), bf16[4,256,2048]{2,1,0:T(8,128)(2,1)}, u32[]{:S(2)}, u32[]{:S(2)}) async-start(bf16[4,256,2048]{2,1,0:T(8,128)(2,1)} %bitcast.132), calls=%async_computation.2 | async-start | bytes 8388608 | tf_op jit(solution)/shard_map/all_to_all | solution.py:162
  429.9 204.0 %all-reduce.5.cloned.1.call-start = ((), (), s32[]{:S(2)}) async-start(), calls=%async_computation.4 | async-start | bytes 4194304 | tf_op jit(solution)/shard_map/psum | solution.py:155
  634.0 4.1 copy-start
Sparse Core Ops, SparseCore 0:
  241.0 133.9 all-reduce.2
  437.0 196.9 all-reduce.4

commit v2 on v1

--- a/solution.py
+++ b/solution.py
@@ -117,9 +117,14 @@
     width = plane // parts
     columns = parts * local_cols
 
+    def of_planes(values, start, size, stride):
+        return jnp.concatenate(
+            [values[:, p * stride + start : p * stride + start + size] for p in range(planes)], 1
+        )
+
     def exchange(values):
-        pieces = values.reshape(2 * local_cols, planes, parts, width).transpose(2, 0, 1, 3)
-        pieces = pieces.reshape(parts, 2 * local_cols, planes * width)
+        values = values.reshape(2 * local_cols, cells)
+        pieces = jnp.stack([of_planes(values, f * width, width, plane) for f in range(parts)], 0)
         pieces = lax.all_to_all(pieces, "freq", split_axis=0, concat_axis=0, tiled=True)
         return pieces.reshape(2 * columns, planes * width)
 
@@ -130,13 +135,16 @@
     low = lax.ppermute(dir_ex[:, (planes - 1) * width :], "space", up)
     high = lax.ppermute(dir_ex[:, :width], "space", [(b, a) for a, b in up])
     over = [(i, i + 1) for i in range(parts - 1)]
-    field = dir_ex.reshape(2 * columns, planes, width)
-    first = field[:, :, :NZ].reshape(2 * columns, planes * NZ)
-    last = field[:, :, width - NZ :].reshape(2 * columns, planes * NZ)
-    before = lax.ppermute(last, "freq", over).reshape(2 * columns, planes, NZ)
+    first = of_planes(dir_ex, 0, NZ, width)
+    last = of_planes(dir_ex, width - NZ, NZ, width)
+    before = lax.ppermute(last, "freq", over)
     after = lax.ppermute(first, "freq", [(b, a) for a, b in over])
-    after = after.reshape(2 * columns, planes, NZ)
-    banded = jnp.concatenate([before, field, after], 2).reshape(2 * columns, -1)
+    bands = []
+    for p in range(planes):
+        bands.append(before[:, p * NZ : (p + 1) * NZ])
+        bands.append(dir_ex[:, p * width : (p + 1) * width])
+        bands.append(after[:, p * NZ : (p + 1) * NZ])
+    banded = jnp.concatenate(bands, 1)
 
     pick = coupling.reshape(7, planes, parts, width)
     pick = lax.dynamic_index_in_dim(pick, mine, 2, False).reshape(7, planes * width)
@@ -159,8 +167,11 @@
     mapping = mapping_of(bal_re, bal_im, parts)
     phi = jnp.dot(mapping, dir_ex, preferred_element_type=jnp.float32).astype(jnp.bfloat16)
     phi = phi.reshape(parts, 2 * local_cols, planes * width)
+    phi, moment = lax.optimization_barrier((phi, moment))
     modes = lax.all_to_all(phi, "freq", split_axis=0, concat_axis=0, tiled=True)
-    modes = modes.reshape(parts, 2 * local_cols, planes, width).transpose(1, 2, 0, 3)
+    modes = jnp.concatenate(
+        [modes[f, :, p * width : (p + 1) * width] for p in range(planes) for f in range(parts)], 1
+    )
     modes = modes.reshape(2, local_cols, cells)
     red_re, red_im = complex_product(
         moment[0], moment[1], bal_re.astype(jnp.float32), bal_im.astype(jnp.float32)

time: 684 us -> 643 us (0.940)
  local copies, waits for them, and re-layouts: 128 us -> 43.4 us
  waiting for transfers between devices: 404 us -> 452 us
  other arithmetic: 38.4 us -> 23.8 us
  starting transfers between devices: 24.2 us -> 36.8 us
    psum x1, waiting for transfers between devices: 203 us -> 115 us  [shards(): moment = lax.psum(moment, ('freq', 'space'))]
    all_to_all x1, waiting for transfers between devices: 0.01 us -> 86.2 us  [shards(): modes = lax.all_to_all(phi, 'freq', split_axis=0, concat_axis=0, tiled=True)]
    reshape x9 -> x0, local copies, waits for them, and re-layouts: 69.8 us -> none  [the longest x2 17.6 us: shards(): modes.reshape(parts, 2 * local_cols, planes, width).transpose(1, 2, 0, 3)]
    all_to_all x2, waiting for transfers between devices: 130 us -> 165 us  [exchange(): lax.all_to_all(pieces, 'freq', split_axis=0, concat_axis=0, tiled=True)]
    another operation x2 -> x0, local copies, waits for them, and re-layouts: 19 us -> none  [shards(): field = dir_ex.reshape(2 * columns, planes, width)]
    add x2, other arithmetic: 18.6 us -> 0.52 us  [conj_moment(): out_re = gram[:, 0, :, :, 0, :] + gram[:, 1, :, :, 1, :]]
    psum x1, waiting for transfers between devices: 69.7 us -> 86.4 us  [shards(): hank = lax.psum(conj_moment(adj_ex, dir_ex, parts), ('freq', 'space'))]
    transpose x2 -> x0, local copies, waits for them, and re-layouts: 14.8 us -> none  [exchange(): values.reshape(2 * local_cols, planes, parts, width).transpose(2, 0, 1, 3)]
  transfers between devices with their start and end apart: 9 -> 9, of which waited for: 4 -> 5; matrix products, arithmetic and copies ran while one was open for 17% -> 11% of each run, Pallas kernels for 2% -> 2%
where the time goes in v2:
time: 643 us; the launch traced here: 635 us
  waiting for transfers between devices  452 us (70%)
  matrix products  47.7 us (7%)
  local copies, waits for them, and re-layouts  43.4 us (7%)
  starting transfers between devices  36.8 us (6%)
  other arithmetic  23.8 us (4%)
  between operations  15.5 us (2%)
  Pallas kernels  15 us (2%)
    all_to_all x2, waiting for transfers between devices, exchange(): lax.all_to_all(pieces, 'freq', split_axis=0, concat_axis=0, tiled=True)  165 us
    psum x1, waiting for transfers between devices, shards(): moment = lax.psum(moment, ('freq', 'space'))  115 us
    psum x1, waiting for transfers between devices, shards(): hank = lax.psum(conj_moment(adj_ex, dir_ex, parts), ('freq', 'space'))  86.4 us
    all_to_all x1, waiting for transfers between devices, shards(): modes = lax.all_to_all(phi, 'freq', split_axis=0, concat_axis=0, tiled=True)  86.2 us
    dot_general x2, matrix products, conj_moment(): lax.dot_general(left, right, (((1,), (1,)), ((), ())), preferred_element_...  15.2 us
    pallas_call x1, Pallas kernels, apply_operator(): pl.pallas_call(lambda *refs: stencil_kernel(planes, width, *refs), out_sh...  15 us
  transfers between devices with their start and end apart: 9, of which 5 were waited for; matrix products, arithmetic and copies ran while one was open for 11% of the time, Pallas kernels for 2%

profile of v2, /device:TPU:0, one launch (start us, length us, event | category | flops | bytes accessed | tf_op | source)
XLA Modules:
  0.0 634.5 jit_solution(3981425464937215601)
XLA Ops:
  7.2 2.6 fusion.82
  10.1 2.2 pad_maximum_fusion.1
  12.3 6.3 all-to-all-start.1
  18.6 2.6 fusion.83
  21.5 2.3 pad_maximum_fusion
  23.8 88.2 %all-to-all-done.1 = bf16[4,256,2048]{2,1,0:T(8,128)(2,1)} async-done(((bf16[4,256,2048]{2,1,0:T(8,128)(2,1)}), bf16[4,256,2048]{2,1,0:T(8,128)(2,1)}, u32[]{:S(2)}, u32[]{:S(2)}) %all-to-all-start.1) | async-done | bytes 4194336 | tf_op jit(solution)/shard_map/all_to_all | solution.py:128
  112.0 4.8 all-to-all-start
  117.5 0.7 select_select_fusion.refs_0_
  118.2 1.4 fusion.81
  119.8 1.3 collective-permute-start.1
  121.2 4.6 collective-permute-start
  125.8 4.0 fusion.80
  129.8 2.6 collective-permute-start.2
  132.4 1.3 collective-permute-start.3
  133.7 76.8 %all-to-all-done = bf16[4,256,2048]{2,1,0:T(8,128)(2,1)} async-done(((bf16[4,256,2048]{2,1,0:T(8,128)(2,1)}), bf16[4,256,2048]{2,1,0:T(8,128)(2,1)}, u32[]{:S(2)}, u32[]{:S(2)}) %all-to-all-start) | async-done | bytes 4194336 | tf_op jit(solution)/shard_map/all_to_all | solution.py:128
  210.5 7.6 %fusion.87 = f32[4,2,128,4,2,128]{5,2,4,3,1,0:T(8,128)S(1)} fusion(bf16[4,2,128,2048,1,1]{3,2,5,4,1,0:T(8,128)(2,1)} %bitcast.7, bf16[4,2,128,2048,1,1]{3,2,1,0,5,4:T(8,128)(2,1)} %bitcast.15), kind=kOutput, calls=%fused_computation.123 | convolution fusion | flops 4294967296 | bytes 12582912 | tf_op jit(solution)/shard_map/dot_general | solution.py:90
  218.3 0.7 copy.17
  219.0 0.7 copy.18
  219.7 3.2 pad_maximum_fusion.2
  222.9 10.9 %all-reduce.5.cloned.1.call-start = ((), (), s32[]{:S(2)}) async-start(), calls=%async_computation.4 | async-start | bytes 4194304 | tf_op jit(solution)/shard_map/psum | solution.py:163
  234.2 9.1 %concatenate.72.refs_2_ = bf16[1024,2304]{1,0:T(8,128)(2,1)} concatenate(bf16[1024,64]{1,0:T(8,128)(2,1)S(1)} %get-tuple-element.49, bf16[1024,1024]{1,0:T(8,128)(2,1)S(1)} %get-tuple-element.21, bf16[1024,64]{1,0:T(8,128)(2,1)S(1)} %get-tuple-element.47, bf16[1024,64]{1,0:T(8,128)(2,1)S(1)} %get-tuple-element.48, bf16[1024,1024]{1,0:T(8,128)(2,1)} %get-tuple-element.20, ...), dimensions={1} | concatenate | bytes 9437184 | tf_op jit(solution)/shard_map/concatenate | solution.py:147
  243.3 15.0 %shard_map.59 = bf16[1024,2048]{1,0:T(8,128)(2,1)} custom-call(f32[7,2048]{1,0:T(8,128)} %select_select_fusion.refs_0_, bf16[1024,2048]{1,0:T(8,128)(2,1)} %bitcast.20.refs_1_, bf16[1024,2304]{1,0:T(8,128)(2,1)} %concatenate.72.refs_2_, bf16[1024,1024]{1,0:T(8,128)(2,1)} %collective-permute-done.2.refs_3_, bf16[1024,1024]{1,0:T(8,128)(2,1)} %collective-permute-done.3.refs_4_), custom_call_target="tpu_custom_call" | custom-call | flops 83886080 | bytes 20971520 | tf_op jit(solution)/shard_map/pallas_call | solution.py:71
  258.3 7.7 %fusion.88 = f32[4,2,128,4,2,128]{5,2,4,3,1,0:T(8,128)S(1)} fusion(bf16[4,2,128,2048,1,1]{3,2,5,4,1,0:T(8,128)(2,1)} %bitcast.7, bf16[4,2,128,2048,1,1]{3,2,1,0,5,4:T(8,128)(2,1)} %bitcast.151), kind=kOutput, calls=%fused_computation.124 | convolution fusion | flops 4294967296 | bytes 12582912 | tf_op jit(solution)/shard_map/dot_general | solution.py:90
  267.6 3.2 pad_maximum_fusion.3
  270.8 86.4 %all-reduce.3.cloned.1.call-done = f32[2,512,512]{2,0,1:T(2,128)} async-done(((f32[2,512,512]{2,0,1:T(2,128)}), f32[2,512,512]{2,0,1:T(2,128)}) %all-reduce.3.cloned.1.call-update) | async-done | bytes 2097168 | tf_op jit(solution)/shard_map/psum | solution.py:160
  357.2 2.1 copy.22
  359.4 1.1 slice.175
  360.5 0.9 fusion.52
  362.1 1.0 fusion.6
  363.1 1.0 fusion.4
  364.2 1.0 select_subtract_fusion.1
  365.2 1.0 fusion
  366.3 1.0 fusion.27
  367.3 1.1 fusion.2
  368.4 1.5 fusion.30
  369.9 1.0 fusion.57
  370.9 1.0 fusion.21
  372.0 1.0 fusion.58
  373.0 1.0 fusion.35
  374.1 1.0 fusion.90
  375.1 1.1 select_subtract_fusion
  376.2 2.0 fusion.89
  378.2 1.1 fusion.37
  379.3 0.8 copy-done.2
  380.1 0.9 reshape.199
  381.0 2.9 copy.23
  383.9 2.1 neg.23
  385.9 3.0 fusion.36
  389.0 1.2 reshape.198
  390.1 2.0 copy.24
  392.2 6.2 maximum_maximum_fusion
  398.3 2.7 reshape.200
  401.0 9.4 %convolution_convert_fusion = bf16[1024,2048]{1,0:T(8,128)(2,1)} fusion(bf16[1024,1024]{1,0:T(8,128)(2,1)} %reshape.200, bf16[1024,2048]{1,0:T(8,128)(2,1)} %bitcast.20.refs_1_), kind=kOutput, calls=%fused_computation.2 | convolution fusion | flops 4297064448 | bytes 10485760 | tf_op jit(solution)/shard_map/dot_general | solution.py:168
  410.4 114.6 %all-reduce.5.cloned.1.call-done = f32[2,512,512]{2,0,1:T(2,128)} async-done(((f32[2,512,512]{2,0,1:T(2,128)}), f32[2,512,512]{2,0,1:T(2,128)}) %all-reduce.5.cloned.1.call-update) | async-done | bytes 2097168 | tf_op jit(solution)/shard_map/psum | solution.py:163
  525.0 5.0 all-to-all-start.2
  530.1 1.6 fusion.84
  531.7 0.7 fusion.42
  532.5 0.8 fusion.34
  533.2 0.7 fusion.40
  534.0 0.8 fusion.33
  534.7 1.6 maximum_multiply_fusion
  536.3 86.2 %all-to-all-done.2 = bf16[4,256,2048]{2,1,0:T(8,128)(2,1)} async-done(((bf16[4,256,2048]{2,1,0:T(8,128)(2,1)}), bf16[4,256,2048]{2,1,0:T(8,128)(2,1)}, u32[]{:S(2)}, u32[]{:S(2)}) %all-to-all-start.2) | async-done | bytes 4194336 | tf_op jit(solution)/shard_map/all_to_all | solution.py:171
  622.5 2.6 fusion.79
  625.5 2.0 copy-done.8
  (54 shorter events, 4.0 us)
Async XLA Ops:
  12.3 99.7 %all-to-all-start.1 = ((bf16[4,256,2048]{2,1,0:T(8,128)(2,1)}), bf16[4,256,2048]{2,1,0:T(8,128)(2,1)}, u32[]{:S(2)}, u32[]{:S(2)}) async-start(bf16[4,256,2048]{2,1,0:T(8,128)(2,1)} %pad_maximum_fusion.1), calls=%async_computation.1 | async-start | bytes 8388608 | tf_op jit(solution)/shard_map/all_to_all | solution.py:128
  23.8 93.1 %copy-start.7 = (f32[7,8192]{1,0:T(8,128)S(1)}, f32[7,8192]{1,0:T(8,128)}, u32[]{:S(2)}) copy-start(f32[7,8192]{1,0:T(8,128)} %param.6) | copy-start | bytes 688132
  23.8 93.5 %copy-start.9 = (s32[8192]{0:T(1024)S(1)}, s32[8192]{0:T(1024)}, u32[]{:S(2)}) copy-start(s32[8192]{0:T(1024)} %param.7) | copy-start | bytes 98308
  112.0 98.4 %all-to-all-start = ((bf16[4,256,2048]{2,1,0:T(8,128)(2,1)}), bf16[4,256,2048]{2,1,0:T(8,128)(2,1)}, u32[]{:S(2)}, u32[]{:S(2)}) async-start(bf16[4,256,2048]{2,1,0:T(8,128)(2,1)} %pad_maximum_fusion), calls=%async_computation | async-start | bytes 8388608 | tf_op jit(solution)/shard_map/all_to_all | solution.py:128
  116.9 240.3 %all-reduce.3.cloned.1.call-start = ((), (), s32[]{:S(2)}) async-start(), calls=%async_computation.3 | async-start | bytes 4194304 | tf_op jit(solution)/shard_map/psum | solution.py:160
  119.8 114.1 %collective-permute-start.1 = (bf16[1024,128]{1,0:T(8,128)(2,1)S(1)}, bf16[1024,128]{1,0:T(8,128)(2,1)S(1)}, u32[]{:S(2)}, u32[]{:S(2)}) collective-permute-start(bf16[1024,128]{1,0:T(8,128)(2,1)S(1)} %pad_maximum_fusion.5), channel_id=1, source_target_pairs={{8,0},{16,8},{24,16},{9,1},{17,9},{25,17},{10,2},{18,10},{26,18},{... | collective-permute-start | bytes 786440 | tf_op jit(solution)/shard_map/ppermute | solution.py:141
  121.2 112.8 %collective-permute-start = (bf16[1024,128]{1,0:T(8,128)(2,1)S(1)}, bf16[1024,128]{1,0:T(8,128)(2,1)S(1)}, u32[]{:S(2)}, u32[]{:S(2)}) collective-permute-start(bf16[1024,128]{1,0:T(8,128)(2,1)S(1)} %pad_maximum_fusion.4), channel_id=1, source_target_pairs={{0,8},{8,16},{16,24},{1,9},{9,17},{17,25},{2,10},{10,18},{18,26},{... | collective-permute-start | bytes 786440 | tf_op jit(solution)/shard_map/ppermute | solution.py:140
  129.8 113.5 %collective-permute-start.2 = (bf16[1024,1024]{1,0:T(8,128)(2,1)}, bf16[1024,1024]{1,0:T(8,128)(2,1)}, u32[]{:S(2)}, u32[]{:S(2)}) collective-permute-start(bf16[1024,1024]{1,0:T(8,128)(2,1)} %get-tuple-element.20), channel_id=1, source_target_pairs={{0,1},{1,2},{2,3},{3,4},{4,5},{5,6},{6,7},{8,9},{9,10},{10,11},{11... | collective-permute-start | bytes 6291464 | tf_op jit(solution)/shard_map/ppermute | solution.py:135
  132.4 110.9 %collective-permute-start.3 = (bf16[1024,1024]{1,0:T(8,128)(2,1)S(1)}, bf16[1024,1024]{1,0:T(8,128)(2,1)}, u32[]{:S(2)}, u32[]{:S(2)}) collective-permute-start(bf16[1024,1024]{1,0:T(8,128)(2,1)S(1)} %get-tuple-element.21), channel_id=1, source_target_pairs={{1,0},{2,1},{3,2},{4,3},{5,4},{6,5},{7,6},{9,8},{10,9},{11,10},{12... | collective-permute-start | bytes 6291464 | tf_op jit(solution)/shard_map/ppermute | solution.py:136
  222.9 302.1 %all-reduce.5.cloned.1.call-start = ((), (), s32[]{:S(2)}) async-start(), calls=%async_computation.4 | async-start | bytes 4194304 | tf_op jit(solution)/shard_map/psum | solution.py:163
  357.2 2.2 copy-start.5
  369.8 8.3 %copy-start = (f32[512,512]{1,0:T(8,128)}, f32[512,512]{1,0:T(8,128)S(1)}, u32[]{:S(2)}) copy-start(f32[512,512]{1,0:T(8,128)S(1)} %fusion.30) | copy-start | bytes 3145732
  379.3 0.8 copy-start.2
  379.3 6.7 %copy-start.1 = (f32[512,512]{1,0:T(8,128)S(1)}, f32[512,512]{1,0:T(8,128)}, u32[]{:S(2)}) copy-start(f32[512,512]{1,0:T(8,128)} %copy-done) | copy-start | bytes 3145732
  525.0 5.0 copy-start.6
  525.0 97.5 %all-to-all-start.2 = ((bf16[4,256,2048]{2,1,0:T(8,128)(2,1)}), bf16[4,256,2048]{2,1,0:T(8,128)(2,1)}, u32[]{:S(2)}, u32[]{:S(2)}) async-start(bf16[4,256,2048]{2,1,0:T(8,128)(2,1)} %bitcast.146), calls=%async_computation.2 | async-start | bytes 8388608 | tf_op jit(solution)/shard_map/all_to_all | solution.py:171
  530.1 1.6 copy-start.4
  530.1 2.4 copy-start.3
  625.5 2.0 copy-start.8
Sparse Core Ops, SparseCore 0:
  223.1 134.0 all-reduce.2
  392.3 132.6 all-reduce.4
